TPU v7x, 256 devices: a whole 4x4x8 slice. The times are simulated.
256 devices in a mesh: replica: 4 (over z_hi), fsdp: 8 (over x, core), tensor: 8 (over y, z_lo).
Axes of the slice: x: 4, y: 4, z: 8 (z_hi: 4, z_lo: 2; z = z_hi * 2 + z_lo), core: 2. Of those that a mesh axis runs over, the one named last changes fastest.
Arguments:
- residual: bfloat16 [8192, 8192], P(('replica', 'fsdp'), 'tensor'), may hold values from -0.6 to 0.6
- norm_gain: bfloat16 [8192], P('tensor'), may hold values from 0.25 to 3.5
- kv_weight: bfloat16 [4, 8192, 6144], P('replica', 'fsdp', 'tensor'), may hold values from -0.0625 to 0.0625
- kv_cotangent: bfloat16 [8192, 6144], P(('replica', 'fsdp'), 'tensor'), may hold values from -0.19921875 to 0.19921875
- frag_local: bfloat16 [4, 8192, 2048], P('replica', 'fsdp', 'tensor'), may hold values from -6 to 6
- frag_base: bfloat16 [8192, 2048], P('fsdp', 'tensor'), may hold values from -6 to 6
- frag_moment: float32 [8192, 2048], P('fsdp', 'tensor'), may hold values from -3 to 3
Outputs:
- residual_grad: bfloat16 [8192, 8192], P(('replica', 'fsdp'), 'tensor')
- kv_weight_grad: float32 [4, 8192, 6144], P('replica', 'fsdp', 'tensor')
- frag_new: bfloat16 [8192, 2048], P('fsdp', 'tensor')
- moment_new: float32 [8192, 2048], P('fsdp', 'tensor')
All inputs are finite; a program needn't handle non-finite values. Where the computation divides by a largest or mean magnitude, that divisor is 1e-20 or more.
Results may differ from a plain program's by a relative error of at most 0.019.
Values may be sent and summed in bfloat16 or wider, within the bound.
A program may use at most 128 MiB of HBM per device.

v0:
```python
import jax
import jax.numpy as jnp
from jax import lax
from jax.sharding import PartitionSpec as P

D = 8192
BLOCK = 128


def local(residual, norm_gain, kv_weight, kv_cotangent, frag_local, frag_base, frag_moment):
    eps = 1e-05
    xf = residual.astype(jnp.float32)
    gain = norm_gain.astype(jnp.float32)
    squares = lax.psum(jnp.sum(xf * xf, axis=-1), "tensor")
    rinv = lax.rsqrt(squares[:, None] / D + eps)
    local_normed = (xf * rinv * gain).astype(jnp.bfloat16)
    normed = lax.all_gather(local_normed, "tensor", axis=1, tiled=True)
    normalized = xf * rinv
    weights = lax.all_gather(kv_weight[0], "fsdp", axis=0, tiled=True)
    head_terms = lax.dot_general(
        kv_cotangent, weights, (((1,), (1,)), ((), ())), preferred_element_type=jnp.float32
    )
    normed_grad = lax.psum_scatter(
        head_terms.astype(jnp.bfloat16), "tensor", scatter_dimension=1, tiled=True
    ).astype(jnp.float32)
    weight_grad = lax.psum_scatter(
        lax.dot_general(
            normed, kv_cotangent, (((0,), (0,)), ((), ())), preferred_element_type=jnp.float32
        ).astype(jnp.bfloat16),
        "fsdp",
        scatter_dimension=0,
        tiled=True,
    ).astype(jnp.float32)
    scaled_grad = gain * normed_grad
    inner = lax.psum(jnp.sum(scaled_grad * normalized, axis=-1), "tensor")
    residual_grad = (rinv * (scaled_grad - normalized * (inner[:, None] / D))).astype(jnp.bfloat16)
    rows_local, cols_local = frag_base.shape
    base = frag_base.astype(jnp.float32)
    delta = base - frag_local[0].astype(jnp.float32)
    blocks = delta.reshape(rows_local, cols_local // BLOCK, BLOCK)
    scales = (jnp.max(jnp.abs(blocks), axis=-1, keepdims=True) + 1e-06).astype(jnp.bfloat16)
    codes = (blocks / scales.astype(jnp.float32)).astype(jnp.bfloat16)
    replicas = lax.axis_size("replica")
    piece_codes = lax.all_gather(codes[None], "replica", axis=0, tiled=True)
    piece_scales = lax.all_gather(scales[None], "replica", axis=0, tiled=True)
    summed = jnp.sum(piece_codes.astype(jnp.float32) * piece_scales.astype(jnp.float32), axis=0)
    outer_grad = (summed / replicas).reshape(rows_local, cols_local)
    moment_new = 0.9 * frag_moment + outer_grad
    frag_new = (base - 0.7 * (outer_grad + 0.9 * moment_new)).astype(jnp.bfloat16)
    return (residual_grad, weight_grad[None], frag_new, moment_new)


def solution(mesh):
    placed = (
        P(("replica", "fsdp"), "tensor"),
        P("tensor"),
        P("replica", "fsdp", "tensor"),
        P(("replica", "fsdp"), "tensor"),
        P("replica", "fsdp", "tensor"),
        P("fsdp", "tensor"),
        P("fsdp", "tensor"),
    )
    return jax.shard_map(
        local,
        mesh=mesh,
        in_specs=placed,
        out_specs=(
            P(("replica", "fsdp"), "tensor"),
            P("replica", "fsdp", "tensor"),
            P("fsdp", "tensor"),
            P("fsdp", "tensor"),
        ),
        check_vma=False,
    )
```

profile of v0, /device:TPU:2, one launch (start us, length us, event | category | flops | bytes accessed | tf_op | source)
XLA Modules:
  0.0 442.4 jit_solution(10433280090311703066)
XLA Ops:
  7.2 0.7 all-gather.10.cloned.1.call-update
  8.0 74.2 %all-gather.10.cloned.1.call-done = bf16[1,8192,768]{2,1,0:T(8,128)(2,1)} async-done(((bf16[1,1024,768]{2,1,0:T(8,128)(2,1)}), bf16[1,8192,768]{2,1,0:T(8,128)(2,1)}) %all-gather.10.cloned.1.call-update) | async-done | bytes 12582928 | tf_op jit(solution)/shard_map/all_gather | solution.py:19
  82.1 14.2 %fusion.2 = bf16[256,8192]{1,0:T(8,128)(2,1)} fusion(bf16[256,768]{1,0:T(8,128)(2,1)S(1)} %copy-done, bf16[1,8192,768]{2,1,0:T(8,128)(2,1)} %all-gather.10.cloned.1.call-done), kind=kOutput, calls=%fused_computation.3 | convolution fusion | flops 3223322624 | bytes 17170432 | tf_op jit(solution)/shard_map/dot_general | solution.py:20
  96.4 0.6 copy-done.5
  97.0 0.4 copy-done.1
  97.5 20.0 %psum.14 = f32[256]{0:T(256)S(1)} all-reduce(f32[256]{0:T(256)S(1)} %fusion.13), channel_id=1, replica_groups=mesh['replica'=4,'fsdp'=8,'tensor'=8] {'tensor'}, use_global_device_ids=true, to_apply=%region_1.0 | all-reduce | flops 256 | bytes 2048 | tf_op jit(solution)/shard_map/psum | solution.py:14
  117.5 73.9 %reduce-scatter.3.cloned.1.call-done = bf16[256,1024]{1,0:T(8,128)(2,1)} async-done(((bf16[256,8192]{1,0:T(8,128)(2,1)}), bf16[256,1024]{1,0:T(8,128)(2,1)}) %reduce-scatter.3.cloned.1.call-update) | async-done | bytes 524304 | tf_op jit(solution)/shard_map/reduce_scatter | solution.py:23
  191.4 1.4 fusion.8
  192.8 17.7 %psum.15 = f32[256]{0:T(256)S(1)} all-reduce(f32[256]{0:T(256)S(1)} %fusion.8), channel_id=1, replica_groups=mesh['replica'=4,'fsdp'=8,'tensor'=8] {'tensor'}, use_global_device_ids=true, to_apply=%region_4.0 | all-reduce | flops 256 | bytes 2048 | tf_op jit(solution)/shard_map/psum | solution.py:35
  210.5 2.4 fusion.12
  213.2 0.2 copy.27
  213.9 1.0 copy.28
  215.0 90.3 %all-gather.6.cloned.1.call-done = bf16[256,8192]{1,0:T(8,128)(2,1)} async-done(((bf16[256,1024]{1,0:T(8,128)(2,1)}), bf16[256,8192]{1,0:T(8,128)(2,1)}) %all-gather.6.cloned.1.call-update) | async-done | bytes 4194320 | tf_op jit(solution)/shard_map/all_gather | solution.py:17
  305.3 10.3 %convolution_convert_fusion = bf16[8192,768]{1,0:T(8,128)(2,1)} fusion(bf16[256,8192]{1,0:T(8,128)(2,1)} %all-gather.6.cloned.1.call-done, bf16[256,768]{1,0:T(8,128)(2,1)S(1)} %copy-done), kind=kOutput, calls=%fused_computation | convolution fusion | flops 3227516928 | bytes 17170432 | tf_op jit(solution)/shard_map/dot_general | solution.py:27
  315.6 16.6 %all-gather.1 = bf16[4096,2]{0,1:T(2,128)(2,1)S(1)} all-gather(bf16[1024,2]{0,1:T(2,128)(2,1)S(1)} %get-tuple-element.17), channel_id=3, replica_groups=mesh['replica'=4,'fsdp'=8,'tensor'=8] {'replica'}, dimensions={0}, use_global_device_ids=true | all-gather | bytes 20480 | tf_op jit(solution)/shard_map/all_gather | solution.py:45
  332.2 0.3 copy.31
  332.6 26.7 %all-gather.8.cloned.1.call-done = bf16[4,1024,2,128]{3,1,2,0:T(8,128)(2,1)} async-done(((bf16[1,1024,2,128]{3,1,2,0:T(8,128)(2,1)}), bf16[4,1024,2,128]{3,1,2,0:T(8,128)(2,1)}) %all-gather.8.cloned.1.call-update) | async-done | bytes 2097168 | tf_op jit(solution)/shard_map/all_gather | solution.py:44
  359.2 2.5 multiply_reduce_fusion
  361.9 1.3 copy.30
  363.2 1.5 bitcast_add_fusion.1
  364.7 1.0 copy.32
  365.7 1.3 copy.33
  367.0 65.5 %reduce-scatter.5.cloned.1.call-done = bf16[1024,768]{1,0:T(8,128)(2,1)} async-done(((bf16[8192,768]{1,0:T(8,128)(2,1)}), bf16[1024,768]{1,0:T(8,128)(2,1)}) %reduce-scatter.5.cloned.1.call-update) | async-done | bytes 1572880 | tf_op jit(solution)/shard_map/reduce_scatter | solution.py:26
  432.6 3.3 bitcast_convert_fusion
  (30 shorter events, 1.2 us)
Async XLA Ops:
  7.2 75.0 %copy-start = (bf16[256,768]{1,0:T(8,128)(2,1)S(1)}, bf16[256,768]{1,0:T(8,128)(2,1)}, u32[]{:S(2)}) copy-start(bf16[256,768]{1,0:T(8,128)(2,1)} %param.10) | copy-start | bytes 1179652
  7.2 74.9 %all-gather.10.cloned.1.call-start = ((), (), s32[]{:S(2)}) async-start(), calls=%async_computation.6 | async-start | bytes 14155776 | tf_op jit(solution)/shard_map/all_gather | solution.py:19
  7.9 183.5 %reduce-scatter.3.cloned.1.call-start = ((), (), s32[]{:S(2)}) async-start(), calls=%async_computation.2 | async-start | bytes 4718592 | tf_op jit(solution)/shard_map/reduce_scatter | solution.py:23
  96.3 0.7 copy-start.5
  96.3 1.1 copy-start.1
  96.3 116.7 %copy-start.3 = (bf16[1024,256]{1,0:T(8,128)(2,1)S(1)}, bf16[1024,256]{1,0:T(8,128)(2,1)}, u32[]{:S(2)}) copy-start(bf16[1024,256]{1,0:T(8,128)(2,1)} %param.12) | copy-start | bytes 1572868
  96.3 116.9 %copy-start.4 = (bf16[1,1024,256]{2,1,0:T(8,128)(2,1)S(1)}, bf16[1,1024,256]{2,1,0:T(8,128)(2,1)}, u32[]{:S(2)}) copy-start(bf16[1,1024,256]{2,1,0:T(8,128)(2,1)} %param.11) | copy-start | bytes 1572868
  96.3 208.9 %all-gather.6.cloned.1.call-start = ((), (), s32[]{:S(2)}) async-start(), calls=%async_computation.3 | async-start | bytes 4718592 | tf_op jit(solution)/shard_map/all_gather | solution.py:17
  212.9 146.3 %all-gather.8.cloned.1.call-start = ((), (), s32[]{:S(2)}) async-start(), calls=%async_computation.5 | async-start | bytes 2621440 | tf_op jit(solution)/shard_map/all_gather | solution.py:44
  214.9 217.7 %reduce-scatter.5.cloned.1.call-start = ((), (), s32[]{:S(2)}) async-start(), calls=%async_computation.4 | async-start | bytes 14155776 | tf_op jit(solution)/shard_map/reduce_scatter | solution.py:26
  315.6 16.7 %copy-start.2 = (f32[1024,256]{1,0:T(8,128)S(1)}, f32[1024,256]{1,0:T(8,128)}, u32[]{:S(2)}) copy-start(f32[1024,256]{1,0:T(8,128)} %param.13) | copy-start | bytes 3145732
Sparse Core Ops, SparseCore 0:
  9.8 72.2 all-gather.9
  96.4 94.9 reduce-scatter.2
  213.0 92.1 all-gather.5
  307.5 51.6 all-gather.7
  361.6 70.8 reduce-scatter.4
where the time goes:
time: 446 us; the launch traced here: 442 us
  waiting for transfers between devices  331 us (74%)
  blocking collectives  54.3 us (12%)
  matrix products  24.4 us (5%)
  between operations  13.9 us (3%)
  other arithmetic  11.8 us (3%)
  local copies, waits for them, and re-layouts  6.35 us (1%)
    all_gather x1, waiting for transfers between devices, local(): normed = lax.all_gather(local_normed, 'tensor', axis=1, tiled=True)  90.3 us
    all_gather x1, waiting for transfers between devices, local(): weights = lax.all_gather(kv_weight[0], 'fsdp', axis=0, tiled=True)  74.2 us
    reduce_scatter x1, waiting for transfers between devices, local(): lax.psum_scatter(head_terms.astype(jnp.bfloat16), 'tensor', scatter_dimen...  73.9 us
    reduce_scatter x1, waiting for transfers between devices, local(): lax.psum_scatter(lax.dot_general(normed, kv_cotangent, (((0,), (0,)), (()...  65.5 us
    all_gather x1, waiting for transfers between devices, local(): piece_codes = lax.all_gather(codes[None], 'replica', axis=0, tiled=True)  26.7 us
    psum x1, blocking collectives, local(): squares = lax.psum(jnp.sum(xf * xf, axis=-1), 'tensor')  20 us
    psum x1, blocking collectives, local(): inner = lax.psum(jnp.sum(scaled_grad * normalized, axis=-1), 'tensor')  17.7 us
    all_gather x1, blocking collectives, local(): piece_scales = lax.all_gather(scales[None], 'replica', axis=0, tiled=True)  16.6 us
  transfers between devices with their start and end apart: 5, of which 5 were waited for; matrix products, arithmetic and copies ran while one was open for 5% of the time, Pallas kernels for 0%

commit v1 on v0

v1 whole, which is shorter than its diff:
```python
import jax
import jax.numpy as jnp
from jax import lax
from jax.experimental import pallas as pl
from jax.experimental.pallas import tpu as pltpu
from jax.sharding import PartitionSpec as P

D = 8192
BLOCK = 128
EPS = 1e-05
TOK = 256
FEAT = 1024
COLS = 768
HALF = FEAT // 2
ROWS = 128
QROWS = 256
F32 = jnp.float32
BF = jnp.bfloat16
MESH = pl.DeviceIdType.MESH
NSEND = 100


def lanes(v):
    out = v[:, :128]
    for i in range(1, v.shape[1] // 128):
        out = out + v[:, i * 128 : (i + 1) * 128]
    return out


def kernel(
    res_hbm, gain_ref, w_hbm, cot_hbm, loc_hbm, base_hbm,
    rg_ref, dw_hbm, fo_hbm,
    res, cot, loc, base, xg, pn, wv, ct, po, ps, pr, cs, cr, ng, dw, dws,
    sq, rcol, sums, inns, fq, fr, fs,
    lsem, ssem, r_sum, r_inn, r_pn, r_pd, r_w, r_ct, r_pr, r_cr, r_ng, r_dw, r_fr, r_fo,
):
    r = lax.axis_index("replica")
    f = lax.axis_index("fsdp")
    t = lax.axis_index("tensor")
    x, c = lax.div(f, 2), lax.rem(f, 2)
    y, zl = lax.div(t, 2), lax.rem(t, 2)

    def dev(x_, c_, y_, z_, r_=r):
        return (r_, x_ * 2 + c_, y_ * 2 + z_)

    def ring(v, o):
        return lax.rem(v + o, 4)

    sib = dev(x, 1 - c, y, zl)
    swap = dev(x, 1 - c, y, 1 - zl)
    up, down = dev(x, c, ring(y, 1), zl), dev(x, c, ring(y, 3), zl)
    xup, xdown, xfar = (dev(ring(x, o), c, y, zl) for o in (1, 3, 2))
    tensors = [(r, f, lax.rem(t + o, 8)) for o in range(1, 8)]
    replicas = [(ring(r, o), f, t) for o in (1, 2, 3)]
    d = ring(y - x + 4, 0)
    straight = c == zl
    crossed = c != zl

    barrier = pltpu.get_barrier_semaphore()
    peers = tensors + replicas + [sib, swap, xup, xdown, xfar]
    for peer in peers:
        pl.semaphore_signal(barrier, inc=1, device_id=peer, device_id_type=MESH)

    loads = [
        pltpu.make_async_copy(src, dst, lsem.at[i])
        for i, (src, dst) in enumerate(((res_hbm, res), (cot_hbm, cot), (loc_hbm, loc), (base_hbm, base)))
    ]
    for load in loads:
        load.start()

    sends = []

    def make(src, dst, sem, device, pred=None):
        cp = pltpu.make_async_remote_copy(
            src_ref=src, dst_ref=dst, send_sem=ssem.at[len(sends)], recv_sem=sem, device_id=device, device_id_type=MESH
        )
        sends.append((pred, cp))
        return cp

    def send(src, dst, sem, device, pred=None):
        cp = make(src, dst, sem, device, pred)
        if pred is None:
            cp.start()
        else:
            pl.when(pred)(cp.start)

    def arrive(ref, sem):
        pltpu.make_async_remote_copy(
            src_ref=ref, dst_ref=ref, send_sem=ssem.at[0], recv_sem=sem, device_id=sib, device_id_type=MESH
        ).wait_recv()

    gain = gain_ref[...].astype(F32)

    loads[0].wait()

    def scale_rows(i, _):
        rows = pl.ds(pl.multiple_of(i * 32, 32), 32)
        v = res[rows, :].astype(F32)
        g = (v * gain).astype(BF)
        xg[0, rows, :] = g[:, :HALF]
        xg[1, rows, :] = g[:, HALF:]
        sq[rows, :] = lanes(v * v)
        return 0

    lax.fori_loop(0, TOK // 32, scale_rows, 0)
    sums[t] = jnp.broadcast_to(jnp.sum(sq[...].T, axis=0, keepdims=True), (8, TOK))

    pl.semaphore_wait(barrier, len(peers))

    for peer in tensors:
        send(sums.at[t], sums.at[t], r_sum.at[t], peer)

    def slot(k):
        return ring(x, (0, 1, 3, 2)[k])

    for q in range(2):
        for h in range(2):
            rows = pl.ds(h * ROWS, ROWS)
            send(xg.at[q, rows], pn.at[x, q, c, rows], r_pn.at[x, q, h], dev(y, c, y, zl), d != 0)

    @pl.when(d == 0)
    def _():
        for q in range(2):
            pn[x, q, c] = xg[q]

    bcast = {}
    for j in range(8):
        xs, q = slot(j // 2), j % 2
        for h in range(2):
            ref = pn.at[xs, q, c, pl.ds(h * ROWS, ROWS)]
            bcast[j, h] = (
                make(ref, ref, r_pn.at[xs, q, h], (up, down)[h], d != (3, 1)[h]),
                lambda ref=ref, xs=xs, q=q, h=h: arrive(ref, r_pn.at[xs, q, h]),
            )

    def b_step(s):
        if s < 8:
            @pl.when(d == 0)
            def _():
                for h in range(2):
                    if s >= 2:
                        bcast[s, h][1]()
                    bcast[s, h][0].start()
        if 0 <= s - 1 < 8:
            for h in range(2):
                @pl.when(d == (1, 3)[h])
                def _():
                    bcast[s - 1, h][1]()
                    bcast[s - 1, h][0].start()
        if 0 <= s - 2 < 8:
            @pl.when(d == 2)
            def _():
                for h in range(2):
                    bcast[s - 2, h][1]()
                    bcast[s - 2, h][0].start()
        if 0 <= s - 3 < 8:
            for h in range(2):
                @pl.when(d == (3, 1)[h])
                def _():
                    bcast[s - 3, h][1]()
            j = s - 3
            ref = pn.at[slot(j // 2), j % 2, c]
            send(ref, ref, r_pd.at[slot(j // 2), j % 2], sib)

    def w_send(q):
        rows = pl.ds(q * HALF, HALF)
        send(w_hbm.at[rows], wv.at[q], r_w.at[q], swap, crossed)

    w_own = [pltpu.make_async_copy(w_hbm.at[pl.ds(q * HALF, HALF)], wv.at[q], r_w.at[q]) for q in range(2)]

    @pl.when(straight)
    def _():
        for q in range(2):
            w_own[q].start()

    b_step(0)
    b_step(1)
    w_send(0)

    loads[1].wait()
    for o in range(1, 8):
        other = lax.rem(t + o, 8)
        arrive(sums.at[other], r_sum.at[other])
    total = jnp.sum(sums[...], axis=0)[0:1]
    rinv = lax.rsqrt(total / D + EPS)
    rcol[...] = jnp.broadcast_to(rinv, (128, TOK)).T

    def scale_cot(i, _):
        rows = pl.ds(pl.multiple_of(i * 32, 32), 32)
        by = rcol[rows, :]
        for l in range(COLS // 128):
            span = slice(l * 128, (l + 1) * 128)
            cot[rows, span] = (cot[rows, span].astype(F32) * by).astype(BF)
        return 0

    lax.fori_loop(0, TOK // 32, scale_cot, 0)
    send(cot, ct.at[x, c], r_ct.at[x, c], dev(x, zl, y, 1 - zl))
    send(cot, ct.at[x, c], r_ct.at[x, c], sib, crossed)

    @pl.when(straight)
    def _():
        ct[x, c] = cot[...]

    w_send(1)
    b_step(2)

    loads[2].wait()
    loads[3].wait()

    def code_rows(i, _):
        rows = pl.ds(pl.multiple_of(i * 64, 64), 64)
        delta = base[rows, :].astype(F32) - loc[rows, :].astype(F32)
        for l in range(2):
            span = slice(l * BLOCK, (l + 1) * BLOCK)
            block = delta[:, span]
            scale = (jnp.max(jnp.abs(block), axis=-1, keepdims=True) + 1e-06).astype(BF).astype(F32)
            code = (block / scale).astype(BF).astype(F32)
            fq[rows, span] = (code * scale).astype(BF)
        return 0

    lax.fori_loop(0, FEAT // 64, code_rows, 0)
    b_step(3)

    def ct_arrive(xs, cc):
        arrive(ct.at[xs, cc], r_ct.at[xs, cc])

    ct_arrive(x, 1 - c)
    pl.when(crossed)(lambda: ct_arrive(x, c))
    for cc in range(2):
        for peer in (xup, xdown):
            send(ct.at[x, cc], ct.at[x, cc], r_ct.at[x, cc], peer)
    b_step(4)
    b_step(5)
    for o in (1, 3, 2):
        rr = ring(r, o)
        send(fq.at[pl.ds(pl.multiple_of(rr * QROWS, QROWS), QROWS)], fr.at[3 - o], r_fr.at[3 - o], (rr, f, t))
    b_step(6)
    b_step(7)

    chain = {}
    for j in range(8):
        for h in range(2):
            chain[j, h] = make(cs.at[j, h], cr.at[j, h], r_cr.at[j, h], (up, down)[h], d != 0)
    final = {}
    for j in range(2, 8):
        for h in range(2):
            q = j % 2
            final[j, h] = make(cs.at[j, h], ng.at[q, h], r_ng.at[q, h], dev(slot(j // 2), c, y, zl), d == 0)

    nt = (((1,), (1,)), ((), ()))
    tn = (((0,), (0,)), ((), ()))

    def a_start(j):
        q, xs = j % 2, slot(j // 2)
        if j < 2:
            arrive_w = pltpu.make_async_copy(wv.at[q], wv.at[q], r_w.at[q])
            arrive_w.wait()
        def part(i, _):
            rows = pl.ds(pl.multiple_of(i * 128, 128), 128)
            ps[j, rows, :] = lax.dot_general(ct[xs, 1 - c, rows, :], wv[q], nt, preferred_element_type=F32).astype(BF)
            return 0
        lax.fori_loop(0, 2, part, 0)
        send(ps.at[j], pr.at[j], r_pr.at[j], sib)
        def mine(i, _):
            rows = pl.ds(pl.multiple_of(i * 128, 128), 128)
            po[j, rows, :] = lax.dot_general(ct[xs, c, rows, :], wv[q], nt, preferred_element_type=F32)
            return 0
        lax.fori_loop(0, 2, mine, 0)

    def a_end(j):
        arrive(pr.at[j], r_pr.at[j])
        for h in range(2):
            rows = pl.ds(h * ROWS, ROWS)
            po[j, rows, :] = po[j, rows, :] + pr[j, rows, :].astype(F32)

            @pl.when(d == (1, 3)[h])
            def _():
                cs[j, h] = po[j, rows, :].astype(BF)
                chain[j, h].start()

    def add(j, h):
        arrive(cr.at[j, h], r_cr.at[j, h])
        return (po[j, pl.ds(h * ROWS, ROWS), :] + cr[j, h].astype(F32)).astype(BF)

    def r_step(s):
        if 0 <= s - 1 < 8:
            j = s - 1

            @pl.when(d == 2)
            def _():
                for h in range(2):
                    cs[j, h] = add(j, h)
                    chain[j, h].start()
        if 0 <= s - 2 < 8:
            i = s - 2
            for h in range(2):
                @pl.when(d == (3, 1)[h])
                def _():
                    cs[i, h] = add(i, h)
                    chain[i, h].start()
        if 0 <= s - 3 < 8:
            k = s - 3

            @pl.when(d == 0)
            def _():
                for h in range(2):
                    if k < 2:
                        ng[k, h] = add(k, h)
                    else:
                        cs[k, h] = add(k, h)
                        final[k, h].start()

    def dw_step(k, q):
        xs = slot(k)
        arrive(pn.at[xs, q, 1 - c], r_pd.at[xs, q])
        right = ct[xs].reshape(2 * TOK, COLS)

        def tile(i, _):
            rows = pl.ds(pl.multiple_of(i * 256, 256), 256)
            left = pn[xs, q, :, :, rows].reshape(2 * TOK, 256)
            part = lax.dot_general(left, right, tn, preferred_element_type=F32)
            if k == 0:
                dw[q, rows, :] = part
            elif k < 3:
                dw[q, rows, :] = dw[q, rows, :] + part
            else:
                dws[q, rows, :] = (dw[q, rows, :] + part).astype(BF)
            return 0

        lax.fori_loop(0, 2, tile, 0)

    a_start(0)
    a_end(0)
    b_step(8)
    r_step(0)
    a_start(1)
    a_end(1)
    b_step(9)
    r_step(1)

    xl, xr = ring(x, 3), ring(x, 1)
    ct_arrive(xl, 0)
    send(ct.at[xl, 0], ct.at[xl, 0], r_ct.at[xl, 0], xup)
    ct_arrive(xr, 1)
    send(ct.at[xr, 1], ct.at[xr, 1], r_ct.at[xr, 1], xdown)
    b_step(10)
    ct_arrive(xr, 0)
    ct_arrive(xl, 1)
    for j in range(2, 6):
        a_start(j)
        a_end(j)
        r_step(j)
        if j >= 4:
            dw_step(0, j - 4)

    for i in range(3):
        arrive(fr.at[i], r_fr.at[i])
    mine = pl.ds(pl.multiple_of(r * QROWS, QROWS), QROWS)

    def code_sum(i, _):
        rows = pl.ds(pl.multiple_of(i * 64, 64), 64)
        own = pl.ds(pl.multiple_of(r * QROWS + i * 64, 64), 64)
        v = fq[own, :].astype(F32)
        for n in range(3):
            v = v + fr[n, rows, :].astype(F32)
        fs[rows, :] = (v * 0.25).astype(BF)
        return 0

    lax.fori_loop(0, QROWS // 64, code_sum, 0)
    keep = pltpu.make_async_copy(fs, fo_hbm.at[mine], lsem.at[4])
    keep.start()
    for o in (1, 3, 2):
        send(fs, fo_hbm.at[mine], r_fo.at[r], (ring(r, o), f, t))

    for k in (1, 2):
        for q in range(2):
            dw_step(k, q)

    far = ring(x, 2)
    ct_arrive(far, 0)
    ct_arrive(far, 1)
    for j in (6, 7):
        a_start(j)
        a_end(j)
        r_step(j)
    w_out = []
    for q in range(2):
        dw_step(3, q)
        rows = pl.ds(q * HALF, HALF)
        send(dws.at[q], dw_hbm.at[rows], r_dw.at[q], swap, crossed)
        w_out.append(pltpu.make_async_copy(dws.at[q], dw_hbm.at[rows], r_dw.at[q]))
        pl.when(straight)(w_out[q].start)
        r_step(8 + q)
    r_step(10)

    def inner_rows(q, i):
        rows = pl.ds(i * 64, 64)
        h, inside = i // 2, pl.ds((i % 2) * 64, 64)
        g = gain[:, q * HALF : (q + 1) * HALF]
        v = ng[q, h, inside, :].astype(F32) * g * res[rows, q * HALF : (q + 1) * HALF].astype(F32)
        if q == 0:
            sq[rows, :] = lanes(v)
        else:
            sq[rows, :] = sq[rows, :] + lanes(v)

    for q in range(2):
        for h in range(2):
            pl.when(d != 0)(lambda q=q, h=h: arrive(ng.at[q, h], r_ng.at[q, h]))
        for i in range(4):
            inner_rows(q, i)
    inns[t] = jnp.broadcast_to(jnp.sum(sq[...].T, axis=0, keepdims=True), (8, TOK))
    for peer in tensors:
        send(inns.at[t], inns.at[t], r_inn.at[t], peer)
    for o in range(1, 8):
        other = lax.rem(t + o, 8)
        arrive(inns.at[other], r_inn.at[other])
    inner = jnp.broadcast_to(jnp.sum(inns[...], axis=0)[0:1] / D, (128, TOK)).T
    rcol[...] = rcol[...] * rcol[...] * inner

    for q in range(2):
        g = gain[:, q * HALF : (q + 1) * HALF]
        for i in range(4):
            rows, h, inside = pl.ds(i * 64, 64), i // 2, pl.ds((i % 2) * 64, 64)
            by = rcol[rows, :]
            for l in range(HALF // 128):
                span = slice(l * 128, (l + 1) * 128)
                full = slice(q * HALF + l * 128, q * HALF + (l + 1) * 128)
                v = ng[q, h, inside, span].astype(F32) * g[:, span] - res[rows, full].astype(F32) * by
                rg_ref[rows, full] = v.astype(BF)

    keep.wait()
    for o in (1, 2, 3):
        rr = ring(r, o)
        arrive(fo_hbm.at[pl.ds(pl.multiple_of(rr * QROWS, QROWS), QROWS)], r_fo.at[rr])
    for q in range(2):
        w_out[q].wait()
    for pred, cp in sends:
        if pred is None:
            cp.wait_send()
        else:
            pl.when(pred)(cp.wait_send)


def local(residual, norm_gain, kv_weight, kv_cotangent, frag_local, frag_base, frag_moment):
    hbm = pl.BlockSpec(memory_space=pl.ANY)
    vmem = pl.BlockSpec(memory_space=pltpu.VMEM)
    dma = pltpu.SemaphoreType.DMA
    residual_grad, weight_grad, outer_grad = pl.pallas_call(
        kernel,
        out_shape=(
            jax.ShapeDtypeStruct((TOK, FEAT), BF),
            jax.ShapeDtypeStruct((FEAT, COLS), BF),
            jax.ShapeDtypeStruct((FEAT, 256), BF),
        ),
        in_specs=[hbm, vmem, hbm, hbm, hbm, hbm],
        out_specs=(vmem, hbm, hbm),
        scratch_shapes=[
            pltpu.VMEM((TOK, FEAT), BF),
            pltpu.VMEM((TOK, COLS), BF),
            pltpu.VMEM((FEAT, 256), BF),
            pltpu.VMEM((FEAT, 256), BF),
            pltpu.VMEM((2, TOK, HALF), BF),
            pltpu.VMEM((4, 2, 2, TOK, HALF), BF),
            pltpu.VMEM((2, HALF, COLS), BF),
            pltpu.VMEM((4, 2, TOK, COLS), BF),
            pltpu.VMEM((8, TOK, HALF), F32),
            pltpu.VMEM((8, TOK, HALF), BF),
            pltpu.VMEM((8, TOK, HALF), BF),
            pltpu.VMEM((8, 2, ROWS, HALF), BF),
            pltpu.VMEM((8, 2, ROWS, HALF), BF),
            pltpu.VMEM((2, 2, ROWS, HALF), BF),
            pltpu.VMEM((2, HALF, COLS), F32),
            pltpu.VMEM((2, HALF, COLS), BF),
            pltpu.VMEM((TOK, 128), F32),
            pltpu.VMEM((TOK, 128), F32),
            pltpu.VMEM((8, 8, TOK), F32),
            pltpu.VMEM((8, 8, TOK), F32),
            pltpu.VMEM((FEAT, 256), BF),
            pltpu.VMEM((3, QROWS, 256), BF),
            pltpu.VMEM((QROWS, 256), BF),
            dma((5,)),
            dma((NSEND,)),
            dma((8,)),
            dma((8,)),
            dma((4, 2, 2)),
            dma((4, 2)),
            dma((2,)),
            dma((4, 2)),
            dma((8,)),
            dma((8, 2)),
            dma((2, 2)),
            dma((2,)),
            dma((3,)),
            dma((4,)),
        ],
        compiler_params=pltpu.CompilerParams(
            collective_id=0, has_side_effects=True, vmem_limit_bytes=52 * 2**20
        ),
        cost_estimate=pl.CostEstimate(flops=6442450944, bytes_accessed=10 * 2**20, transcendentals=0),
    )(residual, norm_gain.reshape(1, FEAT), kv_weight[0], kv_cotangent, frag_local[0], frag_base)
    outer = outer_grad.astype(F32)
    base = frag_base.astype(F32)
    moment_new = 0.9 * frag_moment + outer
    frag_new = (base - 0.7 * (outer + 0.9 * moment_new)).astype(BF)
    return (residual_grad, weight_grad.astype(F32)[None], frag_new, moment_new)


def solution(mesh):
    placed = (
        P(("replica", "fsdp"), "tensor"),
        P("tensor"),
        P("replica", "fsdp", "tensor"),
        P(("replica", "fsdp"), "tensor"),
        P("replica", "fsdp", "tensor"),
        P("fsdp", "tensor"),
        P("fsdp", "tensor"),
    )
    return jax.shard_map(
        local,
        mesh=mesh,
        in_specs=placed,
        out_specs=(
            P(("replica", "fsdp"), "tensor"),
            P("replica", "fsdp", "tensor"),
            P("fsdp", "tensor"),
            P("fsdp", "tensor"),
        ),
        check_vma=False,
    )
```

time: 446 us -> 133 us (0.30)
  waiting for transfers between devices: 331 us -> 0 us
  Pallas kernels: 0 us -> 123 us
  blocking collectives: 54.3 us -> 0 us
  matrix products: 24.4 us -> 0 us
  between operations: 13.9 us -> 0.66 us
  other arithmetic: 11.8 us -> 4.88 us
    all_gather x3 -> x0, waiting for transfers between devices: 191 us -> none  [the longest x1 90.3 us: local(): normed = lax.all_gather(local_normed, 'tensor', axis=1, tiled=True)]
    reduce_scatter x2 -> x0, waiting for transfers between devices: 139 us -> none  [the longest x1 73.9 us: local(): lax.psum_scatter(head_terms.astype(jnp.bfloat16), 'tensor', scatter_dimen...]
    pallas_call x0 -> x1, Pallas kernels: none -> 123 us  [local(): pl.pallas_call(kernel, out_shape=(jax.ShapeDtypeStruct((TOK, FEAT), BF),...]
    psum x2 -> x0, blocking collectives: 37.7 us -> none  [the longest x1 20 us: local(): squares = lax.psum(jnp.sum(xf * xf, axis=-1), 'tensor')]
    dot_general x2 -> x0, matrix products: 24.4 us -> none  [the longest x1 14.2 us: local(): lax.dot_general(kv_cotangent, weights, (((1,), (1,)), ((), ())), preferre...]
    all_gather x1 -> x0, blocking collectives: 16.6 us -> none  [local(): piece_scales = lax.all_gather(scales[None], 'replica', axis=0, tiled=True)]
  transfers between devices with their start and end apart: 5 -> 0, of which waited for: 5 -> 0; matrix products, arithmetic and copies ran while one was open for 5% -> 0% of each run, Pallas kernels for 0% -> 0%
where the time goes in v1:
time: 133 us; the launch traced here: 132 us
  Pallas kernels  123 us (92%)
  other arithmetic  4.88 us (4%)
  local copies, waits for them, and re-layouts  3.53 us (3%)
    pallas_call x1, Pallas kernels, local(): pl.pallas_call(kernel, out_shape=(jax.ShapeDtypeStruct((TOK, FEAT), BF),...  123 us
    broadcast_in_dim x1, other arithmetic, local(): return (residual_grad, weight_grad.astype(F32)[None], frag_new, moment_new)  3.42 us
    unnamed x9, local copies, waits for them, and re-layouts  2.84 us

profile of v1, /device:TPU:2, one launch (start us, length us, event | category | flops | bytes accessed | tf_op | source)
XLA Modules:
  0.0 131.8 jit_solution(7207478700617594339)
XLA Ops:
  0.6 0.7 reshape.11.gain_ref
  1.3 0.0 copy-start
  1.3 1.0 copy-done
  2.4 0.0 copy-start.1
  2.4 1.0 copy-done.1
  3.4 122.7 %shard_map.102 = (bf16[256,1024]{1,0:T(8,128)(2,1)S(1)}, bf16[1024,768]{1,0:T(8,128)(2,1)}, bf16[1024,256]{1,0:T(8,128)(2,1)S(1)}) custom-call(bf16[256,1024]{1,0:T(8,128)(2,1)S(1)} %copy-done, bf16[1,1024]{1,0:T(2,128)(2,1)S(1)} %reshape.11.gain_ref, bf16[1024,768]{1,0:T(8,128)(2,1)} %bitcast.5, bf16[256,768]{1,0:T(8,128)(2,1)S(1)} %copy-done.1, ...), custom_call_target="tpu_custom_call" | custom-call | flops 6442450944 | bytes 10485760 | tf_op jit(solution)/shard_map/pallas_call | solution.py:448
  126.1 0.0 copy-start.2
  126.1 0.0 copy-start.3
  126.1 3.4 %bitcast_convert_fusion = f32[1,1024,768]{2,1,0:T(8,128)} fusion(bf16[1024,768]{1,0:T(8,128)(2,1)} %get-tuple-element.8), kind=kLoop, calls=%fused_computation | loop fusion | flops 786432 | bytes 4718592 | tf_op jit(solution)/shard_map/broadcast_in_dim | solution.py:505
  129.5 0.0 copy-done.2
  129.5 0.0 copy-done.3
  129.5 1.5 %fusion.2 = (bf16[1024,256]{1,0:T(8,128)(2,1)}, f32[1024,256]{1,0:T(8,128)}) fusion(bf16[1024,256]{1,0:T(8,128)(2,1)S(1)} %get-tuple-element.9, bf16[1024,256]{1,0:T(8,128)(2,1)S(1)} %copy-done.3, f32[1024,256]{1,0:T(8,128)S(1)} %copy-done.2), kind=kLoop, calls=%fused_computation.5 | loop fusion | flops 2359296 | bytes 3670016 | tf_op jit(solution)/shard_map/convert_element_type | solution.py:504
  131.0 0.8 copy.12
Async XLA Ops:
  1.3 1.0 copy-start
  2.4 1.0 copy-start.1
  126.1 3.4 %copy-start.2 = (f32[1024,256]{1,0:T(8,128)S(1)}, f32[1024,256]{1,0:T(8,128)}, u32[]{:S(2)}) copy-start(f32[1024,256]{1,0:T(8,128)} %param.13) | copy-start | bytes 3145732
  126.1 3.4 %copy-start.3 = (bf16[1024,256]{1,0:T(8,128)(2,1)S(1)}, bf16[1024,256]{1,0:T(8,128)(2,1)}, u32[]{:S(2)}) copy-start(bf16[1024,256]{1,0:T(8,128)(2,1)} %base_hbm.1) | copy-start | bytes 1572868

commit v2 on v0

v2 whole, which is shorter than its diff:
```python
import jax
import jax.numpy as jnp
from jax import lax
from jax.experimental import pallas as pl
from jax.experimental.pallas import tpu as pltpu
from jax.sharding import PartitionSpec as P

D = 8192
BLOCK = 128
EPS = 1e-05
TOK = 256
FEAT = 1024
COLS = 768
QROWS = 256
F32 = jnp.float32
BF = jnp.bfloat16
MESH = pl.DeviceIdType.MESH
NSEND = 130
LAG = 3


def lanes(v):
    out = v[:, :128]
    for i in range(1, v.shape[1] // 128):
        out = out + v[:, i * 128 : (i + 1) * 128]
    return out


def kernel(
    res_hbm, gain_ref, w_hbm, cot_hbm, loc_hbm, base_hbm,
    rg_ref, dw_hbm, fo_hbm,
    res, cot, loc, base, xg, r1, pn, wv, ct, po, ps, pr, cs, nr, ng, dws,
    sq, rcol, sums, inns, fq, fr, fp, fs,
    lsem, ssem, r_sum, r_inn, r_r1, r_pn, r_pd, r_w, r_ct, r_pr, r_nr, r_dw, r_fr, r_fo,
):
    r = lax.axis_index("replica")
    f = lax.axis_index("fsdp")
    t = lax.axis_index("tensor")
    x, c = lax.div(f, 2), lax.rem(f, 2)
    y, zl = lax.div(t, 2), lax.rem(t, 2)

    def dev(x_, c_, y_, z_, r_=r):
        return (r_, x_ * 2 + c_, y_ * 2 + z_)

    def ring(v, o):
        return lax.rem(v + o, 4)

    sib = dev(x, 1 - c, y, zl)
    swap = dev(x, 1 - c, y, 1 - zl)
    rows_of = [dev(x, c, ring(y, o), zl) for o in range(4)]
    xup, xdown, xfar = (dev(ring(x, o), c, y, zl) for o in (1, 3, 2))
    others = [dev(ring(x, o), c, ring(y, p), zl) for o in (1, 2, 3) for p in (1, 2, 3)]
    tensors = [(r, f, lax.rem(t + o, 8)) for o in range(1, 8)]
    replicas = [(ring(r, o), f, t) for o in (1, 2, 3)]
    d = ring(y - x + 4, 0)
    straight = c == zl
    crossed = c != zl

    barrier = pltpu.get_barrier_semaphore()
    peers = tensors + replicas + others + [sib, swap, xup, xdown, xfar]
    for peer in peers:
        pl.semaphore_signal(barrier, inc=1, device_id=peer, device_id_type=MESH)

    loads = [
        pltpu.make_async_copy(src, dst, lsem.at[i])
        for i, (src, dst) in enumerate(((res_hbm, res), (cot_hbm, cot), (loc_hbm, loc), (base_hbm, base)))
    ]
    for load in loads:
        load.start()

    sends = []

    def make(src, dst, sem, device, pred=None):
        cp = pltpu.make_async_remote_copy(
            src_ref=src, dst_ref=dst, send_sem=ssem.at[len(sends)], recv_sem=sem, device_id=device, device_id_type=MESH
        )
        sends.append((pred, cp))
        return cp

    def send(src, dst, sem, device, pred=None):
        cp = make(src, dst, sem, device, pred)
        if pred is None:
            cp.start()
        else:
            pl.when(pred)(cp.start)

    def arrive(ref, sem):
        pltpu.make_async_remote_copy(
            src_ref=ref, dst_ref=ref, send_sem=ssem.at[0], recv_sem=sem, device_id=sib, device_id_type=MESH
        ).wait_recv()

    gain = jnp.concatenate([gain_ref[i : i + 1, :] for i in range(8)], axis=1).astype(F32)

    loads[0].wait()

    def square_rows(i, _):
        rows = pl.ds(pl.multiple_of(i * 32, 32), 32)
        v = res[rows, :].astype(F32)
        sq[rows, :] = lanes(v * v)
        return 0

    lax.fori_loop(0, TOK // 32, square_rows, 0)
    sums[t] = jnp.broadcast_to(jnp.sum(sq[...].T, axis=0, keepdims=True), (8, TOK))
    loads[1].wait()

    @pl.when(straight)
    def _():
        ct[x, c] = cot[...]

    def slot(k):
        return ring(x, (0, 1, 3, 2)[k])

    def ct_arrive(xs, cc):
        arrive(ct.at[xs, cc], r_ct.at[xs, cc])

    loads[2].wait()
    loads[3].wait()

    def code_rows(i, _):
        rows = pl.ds(pl.multiple_of(i * 64, 64), 64)
        delta = base[rows, :].astype(F32) - loc[rows, :].astype(F32)
        for l in range(2):
            span = slice(l * BLOCK, (l + 1) * BLOCK)
            block = delta[:, span]
            scale = (jnp.max(jnp.abs(block), axis=-1, keepdims=True) + 1e-06).astype(BF).astype(F32)
            code = (block / scale).astype(BF).astype(F32)
            fq[rows, span] = (code * scale).astype(BF)
        return 0

    lax.fori_loop(0, FEAT // 64, code_rows, 0)

    nxt, prv = replicas[0], replicas[2]

    def half_rows(o, h):
        return pl.ds(pl.multiple_of(ring(r, o) * QROWS + h * 128, 128), 128)

    def frag_send():
        send(fq.at[half_rows(2, 0)], fr.at[0], r_fr.at[0], nxt)
        send(fq.at[half_rows(2, 1)], fr.at[1], r_fr.at[1], prv)
        send(fq.at[half_rows(1, 1)], fr.at[2], r_fr.at[2], nxt)
        send(fq.at[half_rows(3, 0)], fr.at[3], r_fr.at[3], prv)

    pl.semaphore_wait(barrier, len(peers))

    for peer in tensors:
        send(sums.at[t], sums.at[t], r_sum.at[t], peer)

    send(cot, ct.at[x, c], r_ct.at[x, c], dev(x, zl, y, 1 - zl))
    send(cot, ct.at[x, c], r_ct.at[x, c], sib, crossed)
    over = []
    for cc in (c, 1 - c):
        ref = ct.at[x, cc]
        over.append([make(ref, ref, r_ct.at[x, cc], peer) for peer in (xup, xdown)])

    @pl.when(straight)
    def _():
        for cp in over[0]:
            cp.start()

    w_own = [pltpu.make_async_copy(w_hbm.at[pl.ds(q * 256, 256)], wv.at[q], r_w.at[q]) for q in range(4)]

    @pl.when(straight)
    def _():
        for q in range(4):
            w_own[q].start()

    for q in range(4):
        send(w_hbm.at[pl.ds(q * 256, 256)], wv.at[q], r_w.at[q], swap, crossed)

    @pl.when(straight)
    def _():
        ct_arrive(x, 1 - c)
        for cp in over[1]:
            cp.start()

    frag_send()

    for o in range(1, 8):
        other = lax.rem(t + o, 8)
        arrive(sums.at[other], r_sum.at[other])
    total = jnp.sum(sums[...], axis=0)[0:1]
    rinv = lax.rsqrt(total / D + EPS)
    rcol[...] = jnp.broadcast_to(rinv, (128, TOK)).T

    def scale_rows(i, _):
        rows = pl.ds(pl.multiple_of(i * 32, 32), 32)
        by = rcol[rows, :]
        for l in range(FEAT // 128):
            span = slice(l * 128, (l + 1) * 128)
            inside = slice(l % 2 * 128, (l % 2 + 1) * 128)
            xg[l // 2, rows, inside] = (res[rows, span].astype(F32) * by * gain[:, span]).astype(BF)
        return 0

    lax.fori_loop(0, TOK // 32, scale_rows, 0)

    r1[0] = xg[0]
    for m in (1, 3, 2):
        send(xg.at[m], r1.at[m], r_r1.at[m], rows_of[m])

    xl, xr = ring(x, 3), ring(x, 1)
    hand = [
        make(ct.at[xl, 0], ct.at[xl, 0], r_ct.at[xl, 0], xup),
        make(ct.at[xr, 1], ct.at[xr, 1], r_ct.at[xr, 1], xdown),
    ]

    def hand_on():
        ct_arrive(xl, 0)
        hand[0].start()
        ct_arrive(xr, 1)
        hand[1].start()

    def columns():
        for m in (1, 3, 2):
            arrive(r1.at[m], r_r1.at[m])
        for o in (1, 3, 2):
            m = ring(d, 4 - o)
            send(r1.at[m], pn.at[m, x, c], r_pn.at[m, x], dev(ring(x, o), c, y, zl))
        pn[d, x, c] = r1[d]

    def spread(k):
        xs = slot(k)
        ref = pn.at[d, xs, c]
        if k:
            arrive(ref, r_pn.at[d, xs])
        for o in (1, 3, 2):
            send(ref, ref, r_pn.at[d, xs], rows_of[o])

    def quarter(i):
        return ring(d, (0, 1, 3, 2)[i])

    def pair(i):
        m = quarter(i)
        if i:
            for k in range(4):
                arrive(pn.at[m, slot(k), c], r_pn.at[m, slot(k)])
        send(pn.at[m, :, c], pn.at[m, :, c], r_pd.at[m], sib)

    nt = (((1,), (1,)), ((), ()))
    tn = (((0,), (0,)), ((), ()))

    def offset(j):
        q, p = j // 4, j % 4
        if q:
            return ring(y, p)
        if p == 3:
            return 2
        o = lax.rem(y + p, 3)
        return o + lax.div(o, 2)

    def a_start(j):
        q, xs = j // 4, ring(x, offset(j))
        right = wv[q]
        ps[j] = lax.dot_general(ct[xs, 1 - c], right, nt, preferred_element_type=F32).astype(BF)
        send(ps.at[j], pr.at[j], r_pr.at[j], sib)
        po[j % 4] = lax.dot_general(ct[xs, c], right, nt, preferred_element_type=F32)

    def a_end(j):
        q, o = j // 4, offset(j)
        arrive(pr.at[j], r_pr.at[j])
        total = (po[j % 4] + pr[j].astype(F32)).astype(BF)
        cs[j] = total
        send(cs.at[j], nr.at[y, q], r_nr.at[y, q], dev(ring(x, o), c, x, zl), d + o != 0)

        @pl.when(d + o == 0)
        def _():
            nr[y, q] = total

    w_out = []

    def dw_step(i):
        m = quarter(i)
        arrive(pn.at[m, :, 1 - c], r_pd.at[m])
        left = pn[m].reshape(8 * TOK, 256)
        right = ct[...].reshape(8 * TOK, COLS)
        dws[m] = lax.dot_general(left, right, tn, preferred_element_type=F32).astype(BF)
        rows = pl.ds(pl.multiple_of(m * 256, 256), 256)
        send(dws.at[m], dw_hbm.at[rows], r_dw.at[m], swap, crossed)
        w_out.append(pltpu.make_async_copy(dws.at[m], dw_hbm.at[rows], r_dw.at[m]))
        pl.when(straight)(w_out[i].start)

    mine = pl.ds(pl.multiple_of(r * QROWS, QROWS), QROWS)
    keep = pltpu.make_async_copy(fs, fo_hbm.at[mine], lsem.at[4])

    def frag_pass():
        for h, o, peer in ((0, 1, nxt), (1, 3, prv)):
            arrive(fr.at[h], r_fr.at[h])
            fp[h] = (fr[h].astype(F32) + fq[half_rows(o, h), :].astype(F32)).astype(BF)
            send(fp.at[h], fr.at[4 + h], r_fr.at[4 + h], peer)

    def frag_sum():
        for h in range(2):
            arrive(fr.at[4 + h], r_fr.at[4 + h])
            arrive(fr.at[3 - h], r_fr.at[3 - h])
            v = fq[half_rows(0, h), :].astype(F32) + fr[4 + h].astype(F32) + fr[3 - h].astype(F32)
            fs[pl.ds(h * 128, 128), :] = (v * 0.25).astype(BF)
        keep.start()
        for h in range(2):
            span = pl.ds(h * 128, 128)
            for peer in (nxt, prv):
                send(fs.at[span], fo_hbm.at[half_rows(0, h)], r_fo.at[r, h], peer)

    def frag_forward():
        for h, o, peer in ((0, 3, nxt), (1, 1, prv)):
            ref, sem = fo_hbm.at[half_rows(o, h)], r_fo.at[ring(r, o), h]
            arrive(ref, sem)
            send(ref, ref, sem, peer)

    def w_arrive(q):
        pltpu.make_async_copy(wv.at[q], wv.at[q], r_w.at[q]).wait()

    columns()
    spread(0)

    @pl.when(crossed)
    def _():
        for cc, cps in zip((c, 1 - c), over):
            ct_arrive(x, cc)
            for cp in cps:
                cp.start()

    pl.when(straight)(hand_on)
    for k in (1, 2, 3):
        spread(k)
    pair(0)
    pl.when(crossed)(hand_on)
    ct_arrive(xr, 0)
    ct_arrive(xl, 1)
    for j in range(16):
        if j == 3:
            ct_arrive(ring(x, 2), 0)
            ct_arrive(ring(x, 2), 1)
        if j % 4 == 0:
            w_arrive(j // 4)
        a_start(j)
        if j == 7:
            dw_step(0)
        if j >= LAG:
            a_end(j - LAG)
        if j == 11:
            frag_pass()
    for j in range(16 - LAG, 16):
        a_end(j)
    pair(1)
    pair(2)
    dw_step(1)
    frag_sum()
    pair(3)
    dw_step(2)
    frag_forward()
    dw_step(3)

    for q in range(4):
        span = slice(q * 256, (q + 1) * 256)
        for p in range(4):
            if p == 0:
                pl.when(d != 0)(lambda q=q: arrive(nr.at[y, q], r_nr.at[y, q]))
            else:
                arrive(nr.at[ring(y, p), q], r_nr.at[ring(y, p), q])

        def inner_rows(i, _):
            rows = pl.ds(pl.multiple_of(i * 32, 32), 32)
            v = nr[0, q, rows, :].astype(F32)
            for p in range(1, 4):
                v = v + nr[p, q, rows, :].astype(F32)
            v = v * gain[:, span]
            ng[rows, span] = v
            v = lanes(v * res[rows, span].astype(F32))
            sq[rows, :] = v if q == 0 else sq[rows, :] + v
            return 0

        lax.fori_loop(0, TOK // 32, inner_rows, 0)
    inns[t] = jnp.broadcast_to(jnp.sum(sq[...].T, axis=0, keepdims=True), (8, TOK))
    for peer in tensors:
        send(inns.at[t], inns.at[t], r_inn.at[t], peer)
    for o in range(1, 8):
        other = lax.rem(t + o, 8)
        arrive(inns.at[other], r_inn.at[other])
    inner = jnp.broadcast_to(jnp.sum(inns[...], axis=0)[0:1] / D, (128, TOK)).T
    sq[...] = rcol[...] * rcol[...] * rcol[...] * inner

    def out_rows(i, _):
        rows = pl.ds(pl.multiple_of(i * 32, 32), 32)
        by, rv = sq[rows, :], rcol[rows, :]
        for l in range(FEAT // 128):
            span = slice(l * 128, (l + 1) * 128)
            rg_ref[rows, span] = (ng[rows, span] * rv - res[rows, span].astype(F32) * by).astype(BF)
        return 0

    lax.fori_loop(0, TOK // 32, out_rows, 0)

    keep.wait()
    for o, h in ((3, 1), (1, 0), (2, 0), (2, 1)):
        arrive(fo_hbm.at[half_rows(o, h)], r_fo.at[ring(r, o), h])
    for i in range(4):
        w_out[i].wait()
    for pred, cp in sends:
        if pred is None:
            cp.wait_send()
        else:
            pl.when(pred)(cp.wait_send)


def finish(dw_ref, outer_ref, base_ref, moment_ref, rg_in, dw_out, frag_out, moment_out, rg_out):
    dw_out[...] = dw_ref[...].astype(F32)
    outer = outer_ref[...].astype(F32)
    moment = 0.9 * moment_ref[...] + outer
    moment_out[...] = moment
    frag_out[...] = (base_ref[...].astype(F32) - 0.7 * (outer + 0.9 * moment)).astype(BF)
    rg_out[...] = rg_in[...]


def local(residual, norm_gain, kv_weight, kv_cotangent, frag_local, frag_base, frag_moment):
    hbm = pl.BlockSpec(memory_space=pl.ANY)
    vmem = pl.BlockSpec(memory_space=pltpu.VMEM)
    dma = pltpu.SemaphoreType.DMA
    residual_grad, weight_grad, outer_grad = pl.pallas_call(
        kernel,
        out_shape=(
            jax.ShapeDtypeStruct((TOK, FEAT), BF),
            jax.ShapeDtypeStruct((FEAT, COLS), BF),
            jax.ShapeDtypeStruct((FEAT, 256), BF),
        ),
        in_specs=[hbm, vmem, hbm, hbm, hbm, hbm],
        out_specs=(vmem, hbm, hbm),
        scratch_shapes=[
            pltpu.VMEM((TOK, FEAT), BF),
            pltpu.VMEM((TOK, COLS), BF),
            pltpu.VMEM((FEAT, 256), BF),
            pltpu.VMEM((FEAT, 256), BF),
            pltpu.VMEM((4, TOK, 256), BF),
            pltpu.VMEM((4, TOK, 256), BF),
            pltpu.VMEM((4, 4, 2, TOK, 256), BF),
            pltpu.VMEM((4, 256, COLS), BF),
            pltpu.VMEM((4, 2, TOK, COLS), BF),
            pltpu.VMEM((4, TOK, 256), F32),
            pltpu.VMEM((16, TOK, 256), BF),
            pltpu.VMEM((16, TOK, 256), BF),
            pltpu.VMEM((16, TOK, 256), BF),
            pltpu.VMEM((4, 4, TOK, 256), BF),
            pltpu.VMEM((TOK, FEAT), F32),
            pltpu.VMEM((4, 256, COLS), BF),
            pltpu.VMEM((TOK, 128), F32),
            pltpu.VMEM((TOK, 128), F32),
            pltpu.VMEM((8, 8, TOK), F32),
            pltpu.VMEM((8, 8, TOK), F32),
            pltpu.VMEM((FEAT, 256), BF),
            pltpu.VMEM((6, 128, 256), BF),
            pltpu.VMEM((2, 128, 256), BF),
            pltpu.VMEM((QROWS, 256), BF),
            dma((5,)),
            dma((NSEND,)),
            dma((8,)),
            dma((8,)),
            dma((4,)),
            dma((4, 4)),
            dma((4,)),
            dma((4,)),
            dma((4, 2)),
            dma((16,)),
            dma((4, 4)),
            dma((4,)),
            dma((6,)),
            dma((4, 2)),
        ],
        compiler_params=pltpu.CompilerParams(
            collective_id=0, has_side_effects=True, vmem_limit_bytes=60 * 2**20
        ),
        cost_estimate=pl.CostEstimate(flops=6442450944, bytes_accessed=10 * 2**20, transcendentals=0),
    )(residual, norm_gain.reshape(8, 128), kv_weight[0], kv_cotangent, frag_local[0], frag_base)
    def rows(n, width):
        return pl.BlockSpec((n, width), lambda i: (i, 0))

    steps = 4
    specs = [rows(FEAT // steps, w) for w in (COLS, 256, 256, 256)] + [rows(TOK // steps, FEAT)]
    weight_grad, frag_new, moment_new, residual_grad = pl.pallas_call(
        finish,
        grid=(steps,),
        out_shape=(
            jax.ShapeDtypeStruct((FEAT, COLS), F32),
            jax.ShapeDtypeStruct((FEAT, 256), BF),
            jax.ShapeDtypeStruct((FEAT, 256), F32),
            jax.ShapeDtypeStruct((TOK, FEAT), BF),
        ),
        in_specs=specs,
        out_specs=(specs[0], specs[1], specs[1], specs[4]),
    )(weight_grad, outer_grad, frag_base, frag_moment, residual_grad)
    return (residual_grad, weight_grad[None], frag_new, moment_new)


def solution(mesh):
    placed = (
        P(("replica", "fsdp"), "tensor"),
        P("tensor"),
        P("replica", "fsdp", "tensor"),
        P(("replica", "fsdp"), "tensor"),
        P("replica", "fsdp", "tensor"),
        P("fsdp", "tensor"),
        P("fsdp", "tensor"),
    )
    return jax.shard_map(
        local,
        mesh=mesh,
        in_specs=placed,
        out_specs=(
            P(("replica", "fsdp"), "tensor"),
            P("replica", "fsdp", "tensor"),
            P("fsdp", "tensor"),
            P("fsdp", "tensor"),
        ),
        check_vma=False,
    )
```

time: 446 us -> 95.4 us (0.21)
  waiting for transfers between devices: 331 us -> 0 us
  Pallas kernels: 0 us -> 94.3 us
  blocking collectives: 54.3 us -> 0 us
  matrix products: 24.4 us -> 0 us
  between operations: 13.9 us -> 0.64 us
  other arithmetic: 11.8 us -> 0 us
  local copies, waits for them, and re-layouts: 6.35 us -> 0 us
    all_gather x3 -> x0, waiting for transfers between devices: 191 us -> none  [the longest x1 90.3 us: local(): normed = lax.all_gather(local_normed, 'tensor', axis=1, tiled=True)]
    reduce_scatter x2 -> x0, waiting for transfers between devices: 139 us -> none  [the longest x1 73.9 us: local(): lax.psum_scatter(head_terms.astype(jnp.bfloat16), 'tensor', scatter_dimen...]
    pallas_call x0 -> x2, Pallas kernels: none -> 94.3 us  [the longest x1 89.4 us: local(): pl.pallas_call(kernel, out_shape=(jax.ShapeDtypeStruct((TOK, FEAT), BF),...]
    psum x2 -> x0, blocking collectives: 37.7 us -> none  [the longest x1 20 us: local(): squares = lax.psum(jnp.sum(xf * xf, axis=-1), 'tensor')]
    dot_general x2 -> x0, matrix products: 24.4 us -> none  [the longest x1 14.2 us: local(): lax.dot_general(kv_cotangent, weights, (((1,), (1,)), ((), ())), preferre...]
    all_gather x1 -> x0, blocking collectives: 16.6 us -> none  [local(): piece_scales = lax.all_gather(scales[None], 'replica', axis=0, tiled=True)]
  transfers between devices with their start and end apart: 5 -> 0, of which waited for: 5 -> 0; matrix products, arithmetic and copies ran while one was open for 5% -> 0% of each run, Pallas kernels for 0% -> 0%
where the time goes in v2:
time: 95.4 us; the launch traced here: 95 us
  Pallas kernels  94.3 us (99%)
    pallas_call x1, Pallas kernels, local(): pl.pallas_call(kernel, out_shape=(jax.ShapeDtypeStruct((TOK, FEAT), BF),...  89.4 us
    pallas_call x1, Pallas kernels, local(): pl.pallas_call(finish, grid=(steps,), out_shape=(jax.ShapeDtypeStruct((FE...  4.96 us

profile of v2, /device:TPU:2, one launch (start us, length us, event | category | flops | bytes accessed | tf_op | source)
XLA Modules:
  0.0 95.0 jit_solution(11451165884501785217)
XLA Ops:
  0.6 89.4 %shard_map.102 = (bf16[256,1024]{1,0:T(8,128)(2,1)}, bf16[1024,768]{1,0:T(8,128)(2,1)}, bf16[1024,256]{1,0:T(8,128)(2,1)}) custom-call(bf16[256,1024]{1,0:T(8,128)(2,1)} %res_hbm.1, bf16[8,128]{1,0:T(8,128)(2,1)} %bitcast.7, bf16[1024,768]{1,0:T(8,128)(2,1)} %bitcast.5, bf16[256,768]{1,0:T(8,128)(2,1)} %cot_hbm.1, bf16[1024,256]{1,0:T(8,128)(2,1)} %bitcast.6, ...), custom_call_target="tpu_custom_call" | custom-call | flops 6442450944 | bytes 10485760 | tf_op jit(solution)/shard_map/pallas_call | solution.py:416
  90.0 5.0 %shard_map.103 = (f32[1024,768]{1,0:T(8,128)}, bf16[1024,256]{1,0:T(8,128)(2,1)}, f32[1024,256]{1,0:T(8,128)}, bf16[256,1024]{1,0:T(8,128)(2,1)}) custom-call(bf16[1024,768]{1,0:T(8,128)(2,1)} %get-tuple-element.11.dw_ref, bf16[1024,256]{1,0:T(8,128)(2,1)} %get-tuple-element.12.outer_ref, bf16[1024,256]{1,0:T(8,128)(2,1)} %base_ref.1, ...), custom_call_target="tpu_custom_call" | custom-call | tf_op jit(solution)/shard_map/pallas_call | solution.py:475

commit v3 on v2

--- a/solution.py
+++ b/solution.py
@@ -97,9 +97,13 @@
         rows = pl.ds(pl.multiple_of(i * 32, 32), 32)
         v = res[rows, :].astype(F32)
         sq[rows, :] = lanes(v * v)
+        g = (v * gain).astype(BF)
+        for m in range(4):
+            xg[m, rows, :] = g[:, m * 256 : (m + 1) * 256]
         return 0
 
     lax.fori_loop(0, TOK // 32, square_rows, 0)
+    r1[0] = xg[0]
     sums[t] = jnp.broadcast_to(jnp.sum(sq[...].T, axis=0, keepdims=True), (8, TOK))
     loads[1].wait()
 
@@ -145,6 +149,9 @@
     for peer in tensors:
         send(sums.at[t], sums.at[t], r_sum.at[t], peer)
 
+    for m in (1, 3, 2):
+        send(xg.at[m], r1.at[m], r_r1.at[m], rows_of[m])
+
     send(cot, ct.at[x, c], r_ct.at[x, c], dev(x, zl, y, 1 - zl))
     send(cot, ct.at[x, c], r_ct.at[x, c], sib, crossed)
     over = []
@@ -173,8 +180,6 @@
         for cp in over[1]:
             cp.start()
 
-    frag_send()
-
     for o in range(1, 8):
         other = lax.rem(t + o, 8)
         arrive(sums.at[other], r_sum.at[other])
@@ -182,21 +187,6 @@
     rinv = lax.rsqrt(total / D + EPS)
     rcol[...] = jnp.broadcast_to(rinv, (128, TOK)).T
 
-    def scale_rows(i, _):
-        rows = pl.ds(pl.multiple_of(i * 32, 32), 32)
-        by = rcol[rows, :]
-        for l in range(FEAT // 128):
-            span = slice(l * 128, (l + 1) * 128)
-            inside = slice(l % 2 * 128, (l % 2 + 1) * 128)
-            xg[l // 2, rows, inside] = (res[rows, span].astype(F32) * by * gain[:, span]).astype(BF)
-        return 0
-
-    lax.fori_loop(0, TOK // 32, scale_rows, 0)
-
-    r1[0] = xg[0]
-    for m in (1, 3, 2):
-        send(xg.at[m], r1.at[m], r_r1.at[m], rows_of[m])
-
     xl, xr = ring(x, 3), ring(x, 1)
     hand = [
         make(ct.at[xl, 0], ct.at[xl, 0], r_ct.at[xl, 0], xup),
@@ -209,13 +199,18 @@
         ct_arrive(xr, 1)
         hand[1].start()
 
+    def times_rinv(m):
+        by = rcol[...]
+        return jnp.concatenate([(r1[m, :, l * 128 : (l + 1) * 128].astype(F32) * by).astype(BF) for l in range(2)], axis=1)
+
     def columns():
         for m in (1, 3, 2):
             arrive(r1.at[m], r_r1.at[m])
         for o in (1, 3, 2):
             m = ring(d, 4 - o)
+            r1[m] = times_rinv(m)
             send(r1.at[m], pn.at[m, x, c], r_pn.at[m, x], dev(ring(x, o), c, y, zl))
-        pn[d, x, c] = r1[d]
+        pn[d, x, c] = times_rinv(d)
 
     def spread(k):
         xs = slot(k)
@@ -238,24 +233,27 @@
     nt = (((1,), (1,)), ((), ()))
     tn = (((0,), (0,)), ((), ()))
 
+    plan = [(0, 0), (0, 1), (0, 2), (1, 0), (1, 1), (1, 2), (0, 3)]
+    plan += [(2, 4 + p) for p in range(4)] + [(1, 3)] + [(3, 4 + p) for p in range(4)]
+
     def offset(j):
-        q, p = j // 4, j % 4
-        if q:
-            return ring(y, p)
+        p = plan[j][1]
+        if p > 3:
+            return ring(y, p - 4)
         if p == 3:
             return 2
         o = lax.rem(y + p, 3)
         return o + lax.div(o, 2)
 
     def a_start(j):
-        q, xs = j // 4, ring(x, offset(j))
+        q, xs = plan[j][0], ring(x, offset(j))
         right = wv[q]
         ps[j] = lax.dot_general(ct[xs, 1 - c], right, nt, preferred_element_type=F32).astype(BF)
         send(ps.at[j], pr.at[j], r_pr.at[j], sib)
         po[j % 4] = lax.dot_general(ct[xs, c], right, nt, preferred_element_type=F32)
 
     def a_end(j):
-        q, o = j // 4, offset(j)
+        q, o = plan[j][0], offset(j)
         arrive(pr.at[j], r_pr.at[j])
         total = (po[j % 4] + pr[j].astype(F32)).astype(BF)
         cs[j] = total
@@ -310,6 +308,7 @@
 
     columns()
     spread(0)
+    frag_send()
 
     @pl.when(crossed)
     def _():
@@ -326,23 +325,25 @@
     ct_arrive(xr, 0)
     ct_arrive(xl, 1)
     for j in range(16):
-        if j == 3:
+        if plan[j] == (0, 3):
             ct_arrive(ring(x, 2), 0)
             ct_arrive(ring(x, 2), 1)
-        if j % 4 == 0:
-            w_arrive(j // 4)
+        if j in (0, 3, 7, 12):
+            w_arrive(plan[j][0])
         a_start(j)
-        if j == 7:
+        if j == 9:
             dw_step(0)
         if j >= LAG:
             a_end(j - LAG)
         if j == 11:
             frag_pass()
+        if j == 10:
+            pair(1)
+        if j == 13:
+            dw_step(1)
     for j in range(16 - LAG, 16):
         a_end(j)
-    pair(1)
     pair(2)
-    dw_step(1)
     frag_sum()
     pair(3)
     dw_step(2)
@@ -470,7 +471,7 @@
     def rows(n, width):
         return pl.BlockSpec((n, width), lambda i: (i, 0))
 
-    steps = 4
+    steps = 2
     specs = [rows(FEAT // steps, w) for w in (COLS, 256, 256, 256)] + [rows(TOK // steps, FEAT)]
     weight_grad, frag_new, moment_new, residual_grad = pl.pallas_call(
         finish,

time: 95.4 us -> 91.2 us (0.956)
  Pallas kernels: 94.3 us -> 90.4 us
    pallas_call x1, Pallas kernels: 89.4 us -> 86.4 us  [local(): pl.pallas_call(kernel, out_shape=(jax.ShapeDtypeStruct((TOK, FEAT), BF),...]
where the time goes in v3:
time: 91.2 us; the launch traced here: 91.1 us
  Pallas kernels  90.4 us (99%)
    pallas_call x1, Pallas kernels, local(): pl.pallas_call(kernel, out_shape=(jax.ShapeDtypeStruct((TOK, FEAT), BF),...  86.4 us
    pallas_call x1, Pallas kernels, local(): pl.pallas_call(finish, grid=(steps,), out_shape=(jax.ShapeDtypeStruct((FE...  4.07 us

profile of v3, /device:TPU:2, one launch (start us, length us, event | category | flops | bytes accessed | tf_op | source)
XLA Modules:
  0.0 91.1 jit_solution(15770505858354587902)
XLA Ops:
  0.6 86.4 %shard_map.102 = (bf16[256,1024]{1,0:T(8,128)(2,1)}, bf16[1024,768]{1,0:T(8,128)(2,1)}, bf16[1024,256]{1,0:T(8,128)(2,1)}) custom-call(bf16[256,1024]{1,0:T(8,128)(2,1)} %res_hbm.1, bf16[8,128]{1,0:T(8,128)(2,1)} %bitcast.7, bf16[1024,768]{1,0:T(8,128)(2,1)} %bitcast.5, bf16[256,768]{1,0:T(8,128)(2,1)} %cot_hbm.1, bf16[1024,256]{1,0:T(8,128)(2,1)} %bitcast.6, ...), custom_call_target="tpu_custom_call" | custom-call | flops 6442450944 | bytes 10485760 | tf_op jit(solution)/shard_map/pallas_call | solution.py:417
  87.0 4.1 %shard_map.103 = (f32[1024,768]{1,0:T(8,128)}, bf16[1024,256]{1,0:T(8,128)(2,1)}, f32[1024,256]{1,0:T(8,128)}, bf16[256,1024]{1,0:T(8,128)(2,1)}) custom-call(bf16[1024,768]{1,0:T(8,128)(2,1)} %get-tuple-element.11.dw_ref, bf16[1024,256]{1,0:T(8,128)(2,1)} %get-tuple-element.12.outer_ref, bf16[1024,256]{1,0:T(8,128)(2,1)} %base_ref.1, ...), custom_call_target="tpu_custom_call" | custom-call | tf_op jit(solution)/shard_map/pallas_call | solution.py:476

commit v4 on v3

--- a/solution.py
+++ b/solution.py
@@ -117,6 +117,53 @@
     def ct_arrive(xs, cc):
         arrive(ct.at[xs, cc], r_ct.at[xs, cc])
 
+    nxt, prv = replicas[0], replicas[2]
+
+    def half_rows(o, h):
+        return pl.ds(pl.multiple_of(ring(r, o) * QROWS + h * 128, 128), 128)
+
+    def frag_send():
+        send(fq.at[half_rows(2, 0)], fr.at[0], r_fr.at[0], nxt)
+        send(fq.at[half_rows(2, 1)], fr.at[1], r_fr.at[1], prv)
+        send(fq.at[half_rows(1, 1)], fr.at[2], r_fr.at[2], nxt)
+        send(fq.at[half_rows(3, 0)], fr.at[3], r_fr.at[3], prv)
+
+    pl.semaphore_wait(barrier, len(peers))
+
+    for peer in tensors:
+        send(sums.at[t], sums.at[t], r_sum.at[t], peer)
+
+    for m in (1, 3, 2):
+        send(xg.at[m], r1.at[m], r_r1.at[m], rows_of[m])
+
+    send(cot, ct.at[x, c], r_ct.at[x, c], dev(x, zl, y, 1 - zl))
+    send(cot, ct.at[x, c], r_ct.at[x, c], sib, crossed)
+    over = []
+    for cc in (c, 1 - c):
+        ref = ct.at[x, cc]
+        over.append([make(ref, ref, r_ct.at[x, cc], peer) for peer in (xup, xdown)])
+
+    @pl.when(straight)
+    def _():
+        for cp in over[0]:
+            cp.start()
+
+    w_own = [pltpu.make_async_copy(w_hbm.at[pl.ds(q * 256, 256)], wv.at[q], r_w.at[q]) for q in range(4)]
+
+    @pl.when(straight)
+    def _():
+        for q in range(4):
+            w_own[q].start()
+
+    for q in range(4):
+        send(w_hbm.at[pl.ds(q * 256, 256)], wv.at[q], r_w.at[q], swap, crossed)
+
+    @pl.when(straight)
+    def _():
+        ct_arrive(x, 1 - c)
+        for cp in over[1]:
+            cp.start()
+
     loads[2].wait()
     loads[3].wait()
 
@@ -132,53 +179,6 @@
         return 0
 
     lax.fori_loop(0, FEAT // 64, code_rows, 0)
-
-    nxt, prv = replicas[0], replicas[2]
-
-    def half_rows(o, h):
-        return pl.ds(pl.multiple_of(ring(r, o) * QROWS + h * 128, 128), 128)
-
-    def frag_send():
-        send(fq.at[half_rows(2, 0)], fr.at[0], r_fr.at[0], nxt)
-        send(fq.at[half_rows(2, 1)], fr.at[1], r_fr.at[1], prv)
-        send(fq.at[half_rows(1, 1)], fr.at[2], r_fr.at[2], nxt)
-        send(fq.at[half_rows(3, 0)], fr.at[3], r_fr.at[3], prv)
-
-    pl.semaphore_wait(barrier, len(peers))
-
-    for peer in tensors:
-        send(sums.at[t], sums.at[t], r_sum.at[t], peer)
-
-    for m in (1, 3, 2):
-        send(xg.at[m], r1.at[m], r_r1.at[m], rows_of[m])
-
-    send(cot, ct.at[x, c], r_ct.at[x, c], dev(x, zl, y, 1 - zl))
-    send(cot, ct.at[x, c], r_ct.at[x, c], sib, crossed)
-    over = []
-    for cc in (c, 1 - c):
-        ref = ct.at[x, cc]
-        over.append([make(ref, ref, r_ct.at[x, cc], peer) for peer in (xup, xdown)])
-
-    @pl.when(straight)
-    def _():
-        for cp in over[0]:
-            cp.start()
-
-    w_own = [pltpu.make_async_copy(w_hbm.at[pl.ds(q * 256, 256)], wv.at[q], r_w.at[q]) for q in range(4)]
-
-    @pl.when(straight)
-    def _():
-        for q in range(4):
-            w_own[q].start()
-
-    for q in range(4):
-        send(w_hbm.at[pl.ds(q * 256, 256)], wv.at[q], r_w.at[q], swap, crossed)
-
-    @pl.when(straight)
-    def _():
-        ct_arrive(x, 1 - c)
-        for cp in over[1]:
-            cp.start()
 
     for o in range(1, 8):
         other = lax.rem(t + o, 8)

time: 91.2 us -> 91.2 us (level)
  no operation moved by 1% of the time
where the time goes in v4:
time: 91.2 us; the launch traced here: 91.1 us
  Pallas kernels  90.4 us (99%)
    pallas_call x1, Pallas kernels, local(): pl.pallas_call(kernel, out_shape=(jax.ShapeDtypeStruct((TOK, FEAT), BF),...  86.4 us
    pallas_call x1, Pallas kernels, local(): pl.pallas_call(finish, grid=(steps,), out_shape=(jax.ShapeDtypeStruct((FE...  4.07 us

profile of v4, /device:TPU:2, one launch (start us, length us, event | category | flops | bytes accessed | tf_op | source)
XLA Modules:
  0.0 91.1 jit_solution(14954292252144602680)
XLA Ops:
  0.6 86.4 %shard_map.102 = (bf16[256,1024]{1,0:T(8,128)(2,1)}, bf16[1024,768]{1,0:T(8,128)(2,1)}, bf16[1024,256]{1,0:T(8,128)(2,1)}) custom-call(bf16[256,1024]{1,0:T(8,128)(2,1)} %res_hbm.1, bf16[8,128]{1,0:T(8,128)(2,1)} %bitcast.7, bf16[1024,768]{1,0:T(8,128)(2,1)} %bitcast.5, bf16[256,768]{1,0:T(8,128)(2,1)} %cot_hbm.1, bf16[1024,256]{1,0:T(8,128)(2,1)} %bitcast.6, ...), custom_call_target="tpu_custom_call" | custom-call | flops 6442450944 | bytes 10485760 | tf_op jit(solution)/shard_map/pallas_call | solution.py:417
  87.0 4.1 %shard_map.103 = (f32[1024,768]{1,0:T(8,128)}, bf16[1024,256]{1,0:T(8,128)(2,1)}, f32[1024,256]{1,0:T(8,128)}, bf16[256,1024]{1,0:T(8,128)(2,1)}) custom-call(bf16[1024,768]{1,0:T(8,128)(2,1)} %get-tuple-element.11.dw_ref, bf16[1024,256]{1,0:T(8,128)(2,1)} %get-tuple-element.12.outer_ref, bf16[1024,256]{1,0:T(8,128)(2,1)} %base_ref.1, ...), custom_call_target="tpu_custom_call" | custom-call | tf_op jit(solution)/shard_map/pallas_call | solution.py:476
